TPU v7x, 32 devices: a whole 2x2x4 slice. The times are simulated.
32 devices in a mesh: groups: 2 (over y), ctx: 4 (over z), head: 2 (over x), user: 2 (over core).
Axes of the slice: x: 2, y: 2, z: 4, core: 2. Of those that a mesh axis runs over, the one named last changes fastest.
Arguments:
- projected: bfloat16 [4, 2048, 8, 4, 128], P(('groups', 'user'), 'ctx', 'head'), parts along dimension 0, may hold values from -6 to 6
- upstream: bfloat16 [4, 2048, 8, 128], P(('groups', 'user'), 'ctx', 'head'), parts along dimension 0, may hold values from -6 to 6
- ips_weight: float32 [4, 2048], P(('groups', 'user')), parts along dimension 0, may hold values from 0.2 to 5
- item_ids: int32 [4, 2048], P(('groups', 'user')), parts along dimension 0, may hold values from 0 to 999
- session_ids: int32 [4, 2048], P(('groups', 'user')), parts along dimension 0, may hold values from 0 to 7, never falling along the last dimension, each value on 1 to 1024 neighbouring positions
- session_blocks: int32 [4, 4, 3], P(('groups', 'user')), parts along dimension 0, may hold values from -1 to 1, as said below
Outputs:
- mixed: bfloat16 [4, 2048, 8, 128], P(('groups', 'user'), 'ctx', 'head'), parts along dimension 0
- proj_grad: bfloat16 [4, 2048, 8, 4, 128], P(('groups', 'user'), 'ctx', 'head'), parts along dimension 0
There are 2 independent parts, one for each index of `groups`. A program takes and returns all parts, laid end to end along the dimension named above; each array names one. Nothing has to cross between parts.
Inputs may be any that keep to these rules, and one draw needn't show every extreme that they name: `session_blocks`: row b lists, in ascending order, distinct blocks below b, and -1 in the remaining slots; row 3 always lists block 1 and never block 2, and row 1 never lists block 0.
All inputs are finite; a program needn't handle non-finite values.
Results may differ from a plain program's by a relative error of at most 0.0056.
Values may be sent and summed in bfloat16 or wider, within the bound.
A program may use at most 128 MiB of HBM per device.

v0:
```python
import jax
import jax.numpy as jnp
from jax import lax
from jax.sharding import PartitionSpec as P

BLOCK = 512


def shifted_2(block, axis, distance):
    devices = range(lax.axis_size(axis))
    route = [(i - distance, i) for i in devices if i - distance in devices]
    return lax.ppermute(block, axis, route)


def pair_scores(queries, keys):
    scale = queries.shape[-1] ** (-0.5)
    return jnp.einsum("ahd,chd->hac", queries, keys, preferred_element_type=jnp.float32) * scale


def attend(queries, keys, values, visible):
    scores = pair_scores(queries, keys)
    probs = jnp.where(visible[None], jax.nn.silu(scores), 0.0).astype(jnp.bfloat16)
    return jnp.einsum("hac,chd->ahd", probs, values, preferred_element_type=jnp.float32)


def attend_back(queries, grad_rows, keys, values, visible):
    scale = queries.shape[-1] ** (-0.5)
    scores = pair_scores(queries, keys)
    sigma = jax.nn.sigmoid(scores)
    probs = jnp.where(visible[None], jax.nn.silu(scores), 0.0).astype(jnp.bfloat16)
    slope = sigma * (1.0 + scores * (1.0 - sigma))
    dprod = jnp.einsum("ahd,chd->hac", grad_rows, values, preferred_element_type=jnp.float32)
    edges = jnp.where(visible[None], dprod * slope, 0.0).astype(jnp.bfloat16)
    grad_q = jnp.einsum("hac,chd->ahd", edges, keys, preferred_element_type=jnp.float32) * scale
    grad_k = jnp.einsum("hac,ahd->chd", edges, queries, preferred_element_type=jnp.float32) * scale
    grad_v = jnp.einsum("hac,ahd->chd", probs, grad_rows, preferred_element_type=jnp.float32)
    return (grad_q, grad_k, grad_v)


def shards(projected, upstream, ips_weight, item_ids, session_ids, session_blocks):
    rows = projected[0]
    count = rows.shape[0]
    heads = rows.shape[1]
    width = rows.shape[3]
    block = BLOCK
    local_blocks = count // block
    ctx_rank = lax.axis_index("ctx")
    first = ctx_rank * local_blocks
    sessions = session_ids[0]
    lists = session_blocks[0]
    gates = rows[:, :, 0]
    queries = rows[:, :, 1].reshape(local_blocks, block, heads, width)
    pairs = rows[:, :, 2:4]
    pair_blocks = pairs.reshape(local_blocks, block, heads, 2, width)
    inner = jnp.arange(block)
    below = inner[None, :] <= inner[:, None]
    everything = jnp.ones((block, block), bool)

    def session_slice(index):
        return lax.dynamic_slice_in_dim(sessions, jnp.maximum(index, 0) * block, block)

    list_rows = []
    local = 0
    glob = first + local
    here = session_slice(glob)
    there = session_slice(glob - 1)
    list_row = lax.dynamic_index_in_dim(lists, glob, 0, keepdims=False)
    prev_listed = jnp.any(list_row == glob - 1)
    own_masks = [below & (here[:, None] == here[None, :])]
    prev_masks = [
        jnp.logical_not(below)
        & (here[:, None] == there[None, :])
        & (glob > 0)
        & jnp.logical_not(prev_listed)
    ]
    list_rows.append(list_row)
    previous = shifted_2(pair_blocks[local_blocks - 1], "ctx", 1)
    prior = [previous] + [pair_blocks[local] for local in range(local_blocks - 1)]
    local = 0
    current = pair_blocks[local]
    total = attend(queries[local], current[:, :, 0], current[:, :, 1], own_masks[local])
    total = total + attend(
        queries[local], prior[local][:, :, 0], prior[local][:, :, 1], prev_masks[local]
    )
    totals = [total]
    piece_blocks = lax.all_gather(pairs, "ctx", axis=0, tiled=True).reshape(
        -1, block, heads, 2, width
    )

    def visit(index, acc):
        chosen = lax.dynamic_index_in_dim(piece_blocks, index, 0, keepdims=False)
        local = 0
        hit = jnp.any(list_rows[local] == index)
        updated = [
            lax.cond(
                hit,
                lambda value, local=local: value
                + attend(queries[local], chosen[:, :, 0], chosen[:, :, 1], everything),
                lambda value: value,
                acc[local],
            )
        ]
        return tuple(updated)

    summed = lax.fori_loop(0, piece_blocks.shape[0], visit, tuple(totals))
    attended = summed[0]
    centre = jnp.mean(attended, -1, keepdims=True)
    shifted = attended - centre
    inv_std = lax.rsqrt(jnp.mean(shifted * shifted, -1, keepdims=True) + 1e-05)
    normed = shifted * inv_std
    gates_f = gates.astype(jnp.float32)
    mixed = (normed * gates_f).astype(jnp.bfloat16)
    weights_row = ips_weight[0]
    items = item_ids[0]
    fresh = jnp.concatenate(
        [(items[1:] != items[:-1]).astype(jnp.float32), jnp.zeros((1,), jnp.float32)]
    )
    scaled = weights_row * fresh * weights_row.shape[0] / jnp.sum(weights_row)
    local_scale = lax.dynamic_slice_in_dim(scaled, ctx_rank * count, count)
    grad_mixed = local_scale[:, None, None] * upstream[0].astype(jnp.float32)
    grad_gates = (grad_mixed * normed).astype(jnp.bfloat16)
    grad_normed = grad_mixed * gates_f
    grad_att = inv_std * (
        grad_normed
        - jnp.mean(grad_normed, -1, keepdims=True)
        - normed * jnp.mean(grad_normed * normed, -1, keepdims=True)
    )
    grad_flat = grad_att.astype(jnp.bfloat16)
    grad_rows = grad_flat.reshape(local_blocks, block, heads, width)
    grad_q = []
    grad_kv = []
    local = 0
    current = pair_blocks[local]
    own_q, own_k, own_v = attend_back(
        queries[local], grad_rows[local], current[:, :, 0], current[:, :, 1], own_masks[local]
    )
    near_q, near_k, near_v = attend_back(
        queries[local],
        grad_rows[local],
        prior[local][:, :, 0],
        prior[local][:, :, 1],
        prev_masks[local],
    )
    grad_q.append(own_q + near_q)
    grad_kv.append(jnp.stack([own_k, own_v], 2))
    backward_prev = jnp.stack([near_k, near_v], 2)
    incoming = shifted_2(backward_prev.astype(jnp.bfloat16), "ctx", -1).astype(jnp.float32)
    grad_kv[local_blocks - 1] = grad_kv[local_blocks - 1] + incoming
    pulled = jnp.stack([rows[:, :, 1], grad_flat], 2)
    piece_pairs = lax.all_gather(pairs, "ctx", axis=0, tiled=True).reshape(
        -1, block, heads, 2, width
    )
    piece_pulled = lax.all_gather(pulled, "ctx", axis=0, tiled=True).reshape(
        -1, block, heads, 2, width
    )

    def visit(index, acc):
        sums, owned = acc
        chosen = lax.dynamic_index_in_dim(piece_pairs, index, 0, keepdims=False)
        asked = lax.dynamic_index_in_dim(piece_pulled, index, 0, keepdims=False)
        target_list = lax.dynamic_index_in_dim(lists, index, 0, keepdims=False)
        local = 0
        hit = jnp.any(list_rows[local] == index)
        new_sums = [
            lax.cond(
                hit,
                lambda value, local=local: value
                + attend_back(
                    queries[local], grad_rows[local], chosen[:, :, 0], chosen[:, :, 1], everything
                )[0],
                lambda value: value,
                sums[local],
            )
        ]
        mine = jnp.any(target_list == first + local)

        def owner_add(value, local=local):
            part_q, part_k, part_v = attend_back(
                asked[:, :, 0],
                asked[:, :, 1],
                pair_blocks[local][:, :, 0],
                pair_blocks[local][:, :, 1],
                everything,
            )
            return value + jnp.stack([part_k, part_v], 2)

        new_owned = [lax.cond(mine, owner_add, lambda value: value, owned[local])]
        return (tuple(new_sums), tuple(new_owned))

    sums, owned = lax.fori_loop(0, piece_pairs.shape[0], visit, (tuple(grad_q), tuple(grad_kv)))
    grad_q = list(sums)
    grad_kv = list(owned)
    grad_q_all = grad_q[0].astype(jnp.bfloat16)
    grad_kv_all = grad_kv[0].astype(jnp.bfloat16)
    result = jnp.concatenate([grad_gates[:, :, None], grad_q_all[:, :, None], grad_kv_all], 2)
    return (mixed[None], result[None])


def solution(mesh):
    placed = (
        P(("groups", "user"), "ctx", "head", None, None),
        P(("groups", "user"), "ctx", "head", None),
        P(("groups", "user"), None),
        P(("groups", "user"), None),
        P(("groups", "user"), None),
        P(("groups", "user"), None, None),
    )
    return jax.shard_map(
        shards,
        mesh=mesh,
        in_specs=placed,
        out_specs=(
            P(("groups", "user"), "ctx", "head", None),
            P(("groups", "user"), "ctx", "head", None, None),
        ),
        check_vma=False,
    )
```

profile of v0, /device:TPU:9, one launch (start us, length us, event | category | flops | bytes accessed | tf_op | source)
XLA Modules:
  0.0 296.4 jit_solution(7141404065452275830)
XLA Ops:
  7.3 2.1 copy.71
  9.4 1.1 slice.88
  10.6 3.2 %collective-permute-start = (bf16[512,4,2,128]{3,0,1,2:T(8,128)(2,1)}, bf16[512,4,2,128]{3,0,1,2:T(8,128)(2,1)S(1)}, u32[]{:S(2)}, u32[]{:S(2)}) collective-permute-start(bf16[512,4,2,128]{3,0,1,2:T(8,128)(2,1)} %slice.88), channel_id=1, source_target_pairs={{0,4},{4,8},{8,12},{1,5},{5,9},{9,13},{2,6},{6,10},{10,14},{3,7},{... | collective-permute-start | bytes 3145736 | tf_op jit(solution)/shard_map/ppermute | solution.py:12
  13.8 0.9 slice.85
  14.9 0.7 compare_reduce_fusion.4
  17.2 0.8 fusion.71
  18.4 3.6 %select_convert_fusion.3 = (bf16[4,512,512]{2,1,0:T(8,128)(2,1)S(1)}, f32[4,512,512]{2,1,0:T(8,128)}) fusion(pred[512,512]{1,0:T(8,128)(4,1)S(1)} %get-tuple-element.484, bf16[512,4,4,128]{3,0,1,2:T(8,128)(2,1)S(1)} %bitcast.218), kind=kOutput, calls=%fused_computation.64 | convolution fusion | flops 275775488 | bytes 7602176 | tf_op jit(solution)/shard_map/ahd,chd->hac/dot_general | solution.py:17
  22.6 41.6 %collective-permute-done = bf16[512,4,2,128]{3,0,1,2:T(8,128)(2,1)S(1)} collective-permute-done((bf16[512,4,2,128]{3,0,1,2:T(8,128)(2,1)}, bf16[512,4,2,128]{3,0,1,2:T(8,128)(2,1)S(1)}, u32[]{:S(2)}, u32[]{:S(2)}) %collective-permute-start) | collective-permute-done | bytes 1048608 | tf_op jit(solution)/shard_map/ppermute | solution.py:12
  64.2 3.6 %select_convert_fusion.2 = (bf16[4,512,512]{2,1,0:T(8,128)(2,1)S(1)}, f32[4,512,512]{2,1,0:T(8,128)}) fusion(pred[512,512]{1,0:T(8,128)(4,1)S(1)} %get-tuple-element.483, bf16[512,4,2,128]{3,0,1,2:T(8,128)(2,1)S(1)} %collective-permute-done, bf16[512,4,4,128]{3,0,1,2:T(8,128)(2,1)S(1)} %bitcast.220), kind=kOutput, calls=%fused_computation.62 | convolution fusion | flops 275775488 | bytes 7602176 | tf_op jit(solution)/shard_map/ahd,chd->hac/dot_general | solution.py:17
  67.8 1.3 copy-done.7
  69.1 0.7 fusion.47
  69.8 36.1 %all-gather.3.cloned.1.call-done = bf16[2048,4,2,128]{3,0,1,2:T(8,128)(2,1)} async-done(((bf16[512,4,2,128]{3,0,1,2:T(8,128)(2,1)}), bf16[2048,4,2,128]{3,0,1,2:T(8,128)(2,1)}) %all-gather.3.cloned.1.call-update) | async-done | bytes 4194320 | tf_op jit(solution)/shard_map/all_gather | solution.py:86
  106.0 4.6 %copy.34 = bf16[4,512,4,2,128]{4,1,2,3,0:T(8,128)(2,1)} copy(bf16[4,512,4,2,128]{4,1,0,2,3:T(8,128)(2,1)} %bitcast.228) | data formatting | bytes 8388608 | tf_op jit(solution)/shard_map/while | solution.py:105
  110.5 5.4 %while.37 = (s32[]{:T(128)}, f32[512,4,128]{2,0,1:T(8,128)S(1)}, s32[3]{0:T(128)S(1)}, bf16[4,512,4,2,128]{4,1,2,3,0:T(8,128)(2,1)}, bf16[512,4,1,128]{3,0,1,2:T(8,128)(2,1)}, /*index=5*/s32[]{:T(128)}) while((s32[]{:T(128)}, f32[512,4,128]{2,0,1:T(8,128)S(1)}, s32[3]{0:T(128)S(1)}, bf16[4,512,4,2,128]{4,1,2,3,0:T(8,128)(2,1)}, ...), condition=%wide.region_5.6_spmd, body=%wide.region_1.5_spmd.sunk | while | flops 543424512 | bytes 5767345 | solution.py:105
  117.0 3.1 %fusion.59 = (f32[512,4]{0,1:T(4,128)S(1)}, f32[512,4]{0,1:T(4,128)S(1)}, bf16[512,4,1,128]{3,0,1,2:T(8,128)(2,1)}) fusion(f32[512]{0:T(512)S(1)} %fusion.71, bf16[512,4,4,128]{3,0,1,2:T(8,128)(2,1)} %bitcast.221, bf16[1,512,4,128]{3,2,1,0:T(4,128)(2,1)} %param.17, f32[512,4]{0,1:T(4,128)S(1)} %add_rsqrt_fusion, f32[512,4,128]{2,0,1:T(8,128)S(1)} %get-tuple-element.405, ...), kind=kLoop, calls=%fused_computation.101 | loop fusion | flops 2879488 | bytes 2656256 | tf_op jit(solution)/shard_map/reduce_sum | solution.py:125
  120.2 3.0 %multiply_convert_fusion.5 = (bf16[512,4,128]{2,0,1:T(8,128)(2,1)S(1)}, bf16[1,512,4,128]{3,1,2,0:T(8,128)(2,1)}) fusion(f32[512,4,128]{2,0,1:T(8,128)S(1)} %get-tuple-element.405, f32[512,4]{0,1:T(4,128)S(1)} %get-tuple-element.489, f32[512,4]{0,1:T(4,128)S(1)} %get-tuple-element.490, f32[512]{0:T(512)S(1)} %fusion.71, f32[512,4]{0,1:T(4,128)S(1)} %add_rsqrt_fusion, ...), kind=kLoop, calls=%fused_computation.91 | loop fusion | flops 3407872 | bytes 3180544 | tf_op jit(solution)/shard_map/convert_element_type | solution.py:128
  123.1 0.8 copy-done.3
  123.9 2.2 pad_maximum_fusion.1
  126.2 2.4 copy.44
  128.7 2.2 copy.49
  130.9 1.8 copy.47
  132.7 0.9 fusion.50
  133.7 3.8 %select_convert_fusion = bf16[4,512,512]{2,1,0:T(8,128)(2,1)S(1)} fusion(f32[4,512,512]{2,1,0:T(8,128)} %get-tuple-element.488, bf16[512,4,128]{2,0,1:T(8,128)(2,1)S(1)} %copy-done.4, pred[512,512]{1,0:T(8,128)(4,1)S(1)} %copy-done.14, bf16[512,4,2,128]{3,0,1,2:T(8,128)(2,1)S(1)} %copy-done.12), kind=kOutput, calls=%fused_computation.60 | convolution fusion | flops 279969792 | bytes 7602176 | tf_op jit(solution)/shard_map/ahd,chd->hac/dot_general | solution.py:32
  137.5 0.9 fusion.49
  138.5 2.1 collective-permute-start.1
  140.6 2.2 select_convert_fusion.1
  142.8 0.9 convolution_bitcast_fusion
  143.8 0.9 fusion.44
  144.7 0.7 fusion.68
  145.4 1.7 fusion.46
  147.1 61.4 %collective-permute-done.1 = bf16[512,4,2,128]{3,0,1,2:T(8,128)(2,1)S(1)} collective-permute-done((bf16[512,4,2,128]{3,0,1,2:T(8,128)(2,1)S(1)}, bf16[512,4,2,128]{3,0,1,2:T(8,128)(2,1)S(1)}, u32[]{:S(2)}, u32[]{:S(2)}) %collective-permute-start.1) | collective-permute-done | bytes 1048608 | tf_op jit(solution)/shard_map/ppermute | solution.py:12
  208.8 27.0 %all-gather.5.cloned.1.call-done = bf16[2048,4,2,128]{3,0,1,2:T(8,128)(2,1)} async-done(((bf16[512,4,2,128]{3,0,1,2:T(8,128)(2,1)}), bf16[2048,4,2,128]{3,0,1,2:T(8,128)(2,1)}) %all-gather.5.cloned.1.call-update) | async-done | bytes 4194320 | tf_op jit(solution)/shard_map/all_gather | solution.py:153
  235.7 4.6 %copy.45 = bf16[4,512,4,2,128]{4,1,2,3,0:T(8,128)(2,1)} copy(bf16[4,512,4,2,128]{4,1,0,2,3:T(8,128)(2,1)} %bitcast.229) | data formatting | bytes 8388608 | tf_op jit(solution)/shard_map/while | solution.py:190
  240.4 40.9 %while.38 = (s32[]{:T(128)}, f32[512,4,128]{2,0,1:T(8,128)}, f32[512,4,2,128]{3,0,1,2:T(8,128)S(1)}, s32[3]{0:T(128)S(1)}, bf16[4,512,4,2,128]{4,1,2,3,0:T(8,128...) while((s32[]{:T(128)}, f32[512,4,128]{2,0,1:T(8,128)}, ...), condition=%wide.region_18.19_spmd, body=%wide.region_11.18_spmd.sunk | while | flops 1908146176 | bytes 45613352 | solution.py:190
  248.3 15.1 %conditional.8 = (f32[512,4,2,128]{3,0,1,2:T(8,128)S(1)}) conditional(s32[]{:T(128)} %convert_element_type.150, f32[512,4,2,128]{3,0,1,2:T(8,128)S(1)} %get-tuple-element.621, (bf16[4,512,4,2,128]{4,1,2,3,0:T(8,128)(2,1)}, s32[]{:T(128)}, bf16[512,4,2,128]{3,0,1,2:T(8,128)(2,1)}, f32[512,4,2,128]{3,0,1,2:T(8,128)S(1)}) %tuple.114), branch_computations={%region_16.16_spmd, %region_17.17_spmd} | conditional | flops 1091829760 | bytes 30408744 | solution.py:187
  248.3 1.3 dynamic-slice_bitcast_fusion.2
  249.6 3.7 %fusion.33 = f32[4,512,512]{2,1,0:T(8,128)} fusion(bf16[512,4,2,128]{3,0,1,2:T(8,128)(2,1)} %get-tuple-element.387, bf16[512,4,2,128]{3,0,1,2:T(8,128)(2,1)S(1)} %dynamic-slice_bitcast_fusion.2), kind=kOutput, calls=%fused_computation.49 | convolution fusion | flops 268435456 | bytes 5242880 | tf_op jit(solution)/shard_map/while/body/eval_jaxpr/cond/branch_1_fun/ahd,chd->hac/dot_general | solution.py:17
  253.4 5.7 %fusion.32 = f32[512,4,1,128]{3,0,1,2:T(8,128)} fusion(f32[4,512,512]{2,1,0:T(8,128)} %fusion.33, bf16[512,4,2,128]{3,0,1,2:T(8,128)(2,1)} %get-tuple-element.387, bf16[512,4,2,128]{3,0,1,2:T(8,128)(2,1)S(1)} %dynamic-slice_bitcast_fusion.2), kind=kOutput, calls=%fused_computation.45 | convolution fusion | flops 547618816 | bytes 6815744 | tf_op jit(solution)/shard_map/while/body/eval_jaxpr/cond/branch_1_fun/hac,ahd->chd/dot_general | solution.py:35
  259.1 3.8 %fusion.30 = f32[512,4,1,128]{3,0,1,2:T(8,128)S(1)} fusion(f32[4,512,512]{2,1,0:T(8,128)} %fusion.33, bf16[512,4,2,128]{3,0,1,2:T(8,128)(2,1)S(1)} %dynamic-slice_bitcast_fusion.2), kind=kOutput, calls=%fused_computation.43 | convolution fusion | flops 274726912 | bytes 5767168 | tf_op jit(solution)/shard_map/while/body/eval_jaxpr/cond/branch_1_fun/hac,ahd->chd/dot_general | solution.py:36
  266.1 15.1 %conditional.8 = (f32[512,4,2,128]{3,0,1,2:T(8,128)S(1)}) conditional(s32[]{:T(128)} %convert_element_type.150, f32[512,4,2,128]{3,0,1,2:T(8,128)S(1)} %get-tuple-element.621, (bf16[4,512,4,2,128]{4,1,2,3,0:T(8,128)(2,1)}, s32[]{:T(128)}, bf16[512,4,2,128]{3,0,1,2:T(8,128)(2,1)}, f32[512,4,2,128]{3,0,1,2:T(8,128)S(1)}) %tuple.114), branch_computations={%region_16.16_spmd, %region_17.17_spmd} | conditional | flops 1091829760 | bytes 30408744 | solution.py:187
  266.1 1.3 dynamic-slice_bitcast_fusion.2
  267.4 3.7 %fusion.33 = f32[4,512,512]{2,1,0:T(8,128)} fusion(bf16[512,4,2,128]{3,0,1,2:T(8,128)(2,1)} %get-tuple-element.387, bf16[512,4,2,128]{3,0,1,2:T(8,128)(2,1)S(1)} %dynamic-slice_bitcast_fusion.2), kind=kOutput, calls=%fused_computation.49 | convolution fusion | flops 268435456 | bytes 5242880 | tf_op jit(solution)/shard_map/while/body/eval_jaxpr/cond/branch_1_fun/ahd,chd->hac/dot_general | solution.py:17
  271.1 5.7 %fusion.32 = f32[512,4,1,128]{3,0,1,2:T(8,128)} fusion(f32[4,512,512]{2,1,0:T(8,128)} %fusion.33, bf16[512,4,2,128]{3,0,1,2:T(8,128)(2,1)} %get-tuple-element.387, bf16[512,4,2,128]{3,0,1,2:T(8,128)(2,1)S(1)} %dynamic-slice_bitcast_fusion.2), kind=kOutput, calls=%fused_computation.45 | convolution fusion | flops 547618816 | bytes 6815744 | tf_op jit(solution)/shard_map/while/body/eval_jaxpr/cond/branch_1_fun/hac,ahd->chd/dot_general | solution.py:35
  276.8 3.8 %fusion.30 = f32[512,4,1,128]{3,0,1,2:T(8,128)S(1)} fusion(f32[4,512,512]{2,1,0:T(8,128)} %fusion.33, bf16[512,4,2,128]{3,0,1,2:T(8,128)(2,1)S(1)} %dynamic-slice_bitcast_fusion.2), kind=kOutput, calls=%fused_computation.43 | convolution fusion | flops 274726912 | bytes 5767168 | tf_op jit(solution)/shard_map/while/body/eval_jaxpr/cond/branch_1_fun/hac,ahd->chd/dot_general | solution.py:36
  281.2 1.6 copy.70
  282.9 1.3 convert_bitcast_fusion
  284.2 0.8 copy.48
  285.0 4.5 %maximum_bitcast_fusion = bf16[1,512,4,4,128]{4,3,2,1,0:T(4,128)(2,1)} fusion(bf16[512,4,2,128]{3,2,1,0:T(2,128)(2,1)S(1)} %copy.70, bf16[512,4,1,128]{3,2,1,0:T(2,128)(2,1)S(1)} %copy.48, bf16[512,4,1,128]{3,2,1,0:T(2,128)(2,1)S(1)} %copy-done.9), kind=kLoop, calls=%fused_computation.67 | loop fusion | flops 6291456 | bytes 4194304 | tf_op jit(solution)/shard_map/broadcast_in_dim | solution.py:196
  (82 shorter events, 13.1 us)
Async XLA Ops:
  7.2 7.5 %copy-start.17 = (s32[1,4,3]{1,0,2:T(1,128)S(1)}, s32[1,4,3]{1,0,2:T(1,128)}, u32[]{:S(2)}) copy-start(s32[1,4,3]{1,0,2:T(1,128)} %param.21) | copy-start | bytes 148
  7.2 9.2 %copy-start.16 = (f32[1,2048]{1,0:T(1,128)S(1)}, f32[1,2048]{1,0:T(1,128)}, u32[]{:S(2)}) copy-start(f32[1,2048]{1,0:T(1,128)} %param.18) | copy-start | bytes 24580
  7.2 9.9 %copy-start.15 = (s32[1,2048]{1,0:T(1,128)S(1)}, s32[1,2048]{1,0:T(1,128)}, u32[]{:S(2)}) copy-start(s32[1,2048]{1,0:T(1,128)} %param.19) | copy-start | bytes 24580
  7.2 10.8 %copy-start.18 = (s32[1,2048]{1,0:T(1,128)S(1)}, s32[1,2048]{1,0:T(1,128)}, u32[]{:S(2)}) copy-start(s32[1,2048]{1,0:T(1,128)} %param.20) | copy-start | bytes 24580
  7.2 98.8 %all-gather.3.cloned.1.call-start = ((), (), s32[]{:S(2)}) async-start(), calls=%async_computation | async-start | bytes 5242880 | tf_op jit(solution)/shard_map/all_gather | solution.py:86
  9.4 54.9 %copy-start.1 = (bf16[1,512,4,4,128]{4,1,2,3,0:T(8,128)(2,1)}, bf16[1,512,4,4,128]{4,1,2,3,0:T(8,128)(2,1)S(1)}, u32[]{:S(2)}) copy-start(bf16[1,512,4,4,128]{4,1,2,3,0:T(8,128)(2,1)S(1)} %copy.71) | copy-start | bytes 6291460
  10.6 225.2 %all-gather.5.cloned.1.call-start = ((), (), s32[]{:S(2)}) async-start(), calls=%async_computation.1 | async-start | bytes 5242880 | tf_op jit(solution)/shard_map/all_gather | solution.py:153
  10.6 53.6 %collective-permute-start = (bf16[512,4,2,128]{3,0,1,2:T(8,128)(2,1)}, bf16[512,4,2,128]{3,0,1,2:T(8,128)(2,1)S(1)}, u32[]{:S(2)}, u32[]{:S(2)}) collective-permute-start(bf16[512,4,2,128]{3,0,1,2:T(8,128)(2,1)} %slice.88), channel_id=1, source_target_pairs={{0,4},{4,8},{8,12},{1,5},{5,9},{9,13},{2,6},{6,10},{10,14},{3,7},{... | collective-permute-start | bytes 3145736 | tf_op jit(solution)/shard_map/ppermute | solution.py:12
  18.4 45.9 %copy-start.13 = (pred[512,512]{1,0:T(8,128)(4,1)}, pred[512,512]{1,0:T(8,128)(4,1)S(1)}, u32[]{:S(2)}) copy-start(pred[512,512]{1,0:T(8,128)(4,1)S(1)} %get-tuple-element.483) | copy-start | bytes 786436
  21.9 45.9 %copy-start.5 = (bf16[4,512,512]{2,1,0:T(8,128)(2,1)}, bf16[4,512,512]{2,1,0:T(8,128)(2,1)S(1)}, u32[]{:S(2)}) copy-start(bf16[4,512,512]{2,1,0:T(8,128)(2,1)S(1)} %get-tuple-element.485) | copy-start | bytes 6291460
  64.2 3.6 %copy-start.11 = (bf16[512,4,2,128]{3,0,1,2:T(8,128)(2,1)}, bf16[512,4,2,128]{3,0,1,2:T(8,128)(2,1)S(1)}, u32[]{:S(2)}) copy-start(bf16[512,4,2,128]{3,0,1,2:T(8,128)(2,1)S(1)} %collective-permute-done) | copy-start | bytes 3145732
  67.8 1.3 copy-start.7
  116.0 4.2 %copy-start.2 = (bf16[1,512,4,4,128]{4,1,2,3,0:T(8,128)(2,1)S(1)}, bf16[1,512,4,4,128]{4,1,2,3,0:T(8,128)(2,1)}, u32[]{:S(2)}) copy-start(bf16[1,512,4,4,128]{4,1,2,3,0:T(8,128)(2,1)} %copy-done.1) | copy-start | bytes 6291460
  123.1 0.8 copy-start.3
  123.1 7.8 %copy-start.10 = (bf16[512,4,1,128]{3,0,1,2:T(8,128)(2,1)S(1)}, bf16[512,4,1,128]{3,0,1,2:T(8,128)(2,1)}, u32[]{:S(2)}) copy-start(bf16[512,4,1,128]{3,0,1,2:T(8,128)(2,1)} %get-tuple-element.480) | copy-start | bytes 1572868
  126.1 6.6 %copy-start.4 = (bf16[512,4,128]{2,0,1:T(8,128)(2,1)S(1)}, bf16[512,4,128]{2,0,1:T(8,128)(2,1)}, u32[]{:S(2)}) copy-start(bf16[512,4,128]{2,0,1:T(8,128)(2,1)} %copy-done.3) | copy-start | bytes 1572868
  126.2 6.5 %copy-start.8 = (bf16[4,512,512]{2,1,0:T(8,128)(2,1)S(1)}, bf16[4,512,512]{2,1,0:T(8,128)(2,1)}, u32[]{:S(2)}) copy-start(bf16[4,512,512]{2,1,0:T(8,128)(2,1)} %copy-done.7) | copy-start | bytes 6291460
  126.2 7.4 %copy-start.12 = (bf16[512,4,2,128]{3,0,1,2:T(8,128)(2,1)S(1)}, bf16[512,4,2,128]{3,0,1,2:T(8,128)(2,1)}, u32[]{:S(2)}) copy-start(bf16[512,4,2,128]{3,0,1,2:T(8,128)(2,1)} %copy-done.11) | copy-start | bytes 3145732
  126.2 7.4 %copy-start.14 = (pred[512,512]{1,0:T(8,128)(4,1)S(1)}, pred[512,512]{1,0:T(8,128)(4,1)}, u32[]{:S(2)}) copy-start(pred[512,512]{1,0:T(8,128)(4,1)} %copy-done.13) | copy-start | bytes 786436
  137.5 3.1 %copy-start.19 = (f32[4,512,512]{2,1,0:T(8,128)S(1)}, f32[4,512,512]{2,1,0:T(8,128)}, u32[]{:S(2)}) copy-start(f32[4,512,512]{2,1,0:T(8,128)} %get-tuple-element.486) | copy-start | bytes 12582916
  138.5 70.0 %collective-permute-start.1 = (bf16[512,4,2,128]{3,0,1,2:T(8,128)(2,1)S(1)}, bf16[512,4,2,128]{3,0,1,2:T(8,128)(2,1)S(1)}, u32[]{:S(2)}, u32[]{:S(2)}) collective-permute-start(bf16[512,4,2,128]{3,0,1,2:T(8,128)(2,1)S(1)} %pad_maximum_fusion), channel_id=1, source_target_pairs={{4,0},{8,4},{12,8},{5,1},{9,5},{13,9},{6,2},{10,6},{14,10},{7,3},{... | collective-permute-start | bytes 3145736 | tf_op jit(solution)/shard_map/ppermute | solution.py:12
  140.6 2.3 copy-start.6
  259.1 3.8 %copy-start = (f32[512,4,1,128]{3,0,1,2:T(8,128)S(1)}, f32[512,4,1,128]{3,0,1,2:T(8,128)}, u32[]{:S(2)}) copy-start(f32[512,4,1,128]{3,0,1,2:T(8,128)} %fusion.32) | copy-start | bytes 3145732 | tf_op jit(solution)/shard_map/while/body/eval_jaxpr/cond
  276.8 3.8 %copy-start = (f32[512,4,1,128]{3,0,1,2:T(8,128)S(1)}, f32[512,4,1,128]{3,0,1,2:T(8,128)}, u32[]{:S(2)}) copy-start(f32[512,4,1,128]{3,0,1,2:T(8,128)} %fusion.32) | copy-start | bytes 3145732 | tf_op jit(solution)/shard_map/while/body/eval_jaxpr/cond
  281.2 3.8 %copy-start.9 = (bf16[512,4,1,128]{3,2,1,0:T(2,128)(2,1)S(1)}, bf16[512,4,1,128]{3,2,1,0:T(2,128)(2,1)}, u32[]{:S(2)}) copy-start(bf16[512,4,1,128]{3,2,1,0:T(2,128)(2,1)} %copy.47) | copy-start | bytes 1572868
Sparse Core Ops, SparseCore 0:
  10.7 95.2 all-gather.2
  126.2 109.4 all-gather.4
where the time goes:
time: 297 us; the launch traced here: 296 us
  waiting for transfers between devices  166 us (56%)
  matrix products  47.1 us (16%)
  local copies, waits for them, and re-layouts  27.4 us (9%)
  other arithmetic  27.3 us (9%)
  between operations  15 us (5%)
  loops' own time  8.06 us (3%)
  starting transfers between devices  5.34 us (2%)
    ppermute x2, waiting for transfers between devices, shifted_2(): return lax.ppermute(block, axis, route)  103 us
    all_gather x1, waiting for transfers between devices, shards(): lax.all_gather(pairs, 'ctx', axis=0, tiled=True)  36.1 us
    all_gather x1, waiting for transfers between devices, shards(): lax.all_gather(pulled, 'ctx', axis=0, tiled=True)  27 us
    dot_general x4, matrix products, pair_scores(): jnp.einsum('ahd,chd->hac', queries, keys, preferred_element_type=jnp.floa...  14.6 us
    dot_general x4, matrix products, attend_back(): jnp.einsum('hac,ahd->chd', edges, queries, preferred_element_type=jnp.flo...  13.3 us
    dot_general x4, matrix products, attend_back(): jnp.einsum('hac,ahd->chd', probs, grad_rows, preferred_element_type=jnp.f...  9.45 us
    while x3, local copies, waits for them, and re-layouts, shards(): lax.fori_loop(0, piece_pairs.shape[0], visit, (tuple(grad_q), tuple(grad_...  8.68 us
    unnamed x41, local copies, waits for them, and re-layouts  6.66 us
  transfers between devices with their start and end apart: 4, of which 4 were waited for; matrix products, arithmetic and copies ran while one was open for 11% of the time, Pallas kernels for 0%

commit v1 on v0

--- a/solution.py
+++ b/solution.py
@@ -1,6 +1,9 @@
+import functools
 import jax
 import jax.numpy as jnp
 from jax import lax
+from jax.experimental import pallas as pl
+from jax.experimental.pallas import tpu as pltpu
 from jax.sharding import PartitionSpec as P
 
 BLOCK = 512
@@ -196,7 +199,380 @@
     return (mixed[None], result[None])
 
 
+MESH = pl.DeviceIdType.MESH
+NT = (((1,), (1,)), ((), ()))
+TN = (((0,), (0,)), ((), ()))
+NN = (((1,), (0,)), ((), ()))
+
+
+def dot(a, b, dims):
+    return lax.dot_general(a, b, dims, preferred_element_type=jnp.float32)
+
+
+def four_kernel(
+    heads,
+    proj,
+    up,
+    cvec,
+    sess_row,
+    sess_col,
+    listed,
+    mixed,
+    grads,
+    qb,
+    kb,
+    gb,
+    yin,
+    yout,
+    dqin,
+    dqout,
+    dkvin,
+    dkvout,
+    ptab,
+    stab,
+    mask,
+    yown,
+    acc,
+    dkv,
+    dkvown,
+    q_sem,
+    y_sem,
+    g_sem,
+    dq_sem,
+    kv_sem,
+    dkv_sem,
+):
+    me = lax.axis_index("ctx")
+    block, width = up.shape[1], up.shape[2]
+    scale = width ** (-0.5)
+    half = block // 2
+    n_q = jnp.where(me == 1, 3, jnp.where(me == 2, 2, 1))
+    n_kv = jnp.where(me == 1, 2, 1)
+
+    barrier = pltpu.get_barrier_semaphore()
+    for d in range(1, 4):
+        pl.semaphore_signal(
+            barrier, inc=1, device_id={"ctx": lax.rem(me + d, 4)}, device_id_type=MESH
+        )
+    pl.semaphore_wait(barrier, 3)
+
+    def remote(src, dst, sem, slot, h, to):
+        return pltpu.make_async_remote_copy(
+            src_ref=src,
+            dst_ref=dst,
+            send_sem=sem.at[0, slot, h],
+            recv_sem=sem.at[1, slot, h],
+            device_id={"ctx": to},
+            device_id_type=MESH,
+        )
+
+    def q_copy(d, h):
+        return remote(proj.at[h, 1], qb.at[d, h], q_sem, d - 1, h, lax.rem(me + 4 - d, 4))
+
+    def g_copy(d, h):
+        return remote(gb.at[0, h], gb.at[d, h], g_sem, d - 1, h, lax.rem(me + 4 - d, 4))
+
+    def y_copy(d, h):
+        return remote(yout.at[d - 1, h], yin.at[d - 1, h], y_sem, d - 1, h, lax.rem(me + d, 4))
+
+    def dq_copy(d, h):
+        return remote(dqout.at[d - 1, h], dqin.at[d - 1, h], dq_sem, d - 1, h, lax.rem(me + d, 4))
+
+    def kv_copy(h):
+        return remote(proj.at[h, pl.ds(2, 2)], kb.at[1, h], kv_sem, 0, h, lax.rem(me + 1, 4))
+
+    def dkv_copy(h):
+        return remote(dkvout.at[h], dkvin.at[h], dkv_sem, 0, h, lax.rem(me + 3, 4))
+
+    asks = {1: me >= 2, 2: me == 3}
+    helps = {1: (me == 1) | (me == 2), 2: me == 1}
+
+    for h in range(heads):
+        for d in (2, 1):
+
+            @pl.when(asks[d])
+            def _():
+                q_copy(d, h).start()
+
+        @pl.when(me == 0)
+        def _():
+            kv_copy(h).start()
+
+    qb[0] = proj[:, 1]
+    kb[0] = proj[:, 2:4]
+
+    def fill(pair, carry):
+        qi, kj = pair // 2, lax.rem(pair, 2)
+
+        @pl.when((qi < n_q) & (kj < n_kv))
+        def _():
+            bq, bk = me + qi, me - kj
+            row = sess_row[bq]
+            gap = bq - bk
+            full = listed[bq * 4 + bk]
+            for t in range(2):
+                col = sess_col[bk, pl.ds(t * half, half)]
+                c = lax.broadcasted_iota(jnp.int32, (half, block), 0) + t * half
+                a = lax.broadcasted_iota(jnp.int32, (half, block), 1)
+                ahead = a - c + gap * block
+                window = (ahead >= 0) & (ahead < block)
+                near = jnp.where(window & (row == col), 1.0, 0.0)
+                mask[pair, pl.ds(t * half, half)] = jnp.maximum(near, full)
+
+        return carry
+
+    lax.fori_loop(0, 6, fill, 0)
+
+    def forward(h, carry):
+        @pl.when(me == 1)
+        def _():
+            kv_copy(h).wait_recv()
+
+        def one_q(qi, carry):
+            for d in (1, 2):
+
+                @pl.when((qi == d) & helps[d])
+                def _():
+                    q_copy(d, h).wait_recv()
+
+            acc[...] = jnp.zeros_like(acc)
+            query = qb[qi, h]
+
+            def one_k(kj, carry):
+                pair = qi * 2 + kj
+                for t in range(2):
+                    part = pl.ds(t * half, half)
+                    raw = dot(kb[kj, h, 0, part], query, NT)
+                    sigma = 0.5 * jnp.tanh(raw * (0.5 * scale)) + 0.5
+                    prob = raw * scale * sigma
+                    slope = sigma + prob * (1.0 - sigma)
+                    seen = mask[pair, part]
+                    prob = (prob * seen).astype(jnp.bfloat16)
+                    ptab[pair, h, part] = prob
+                    stab[pair, h, part] = (slope * seen).astype(jnp.bfloat16)
+                    acc[...] += dot(kb[kj, h, 1, part], prob, TN)
+                return carry
+
+            lax.fori_loop(0, n_kv, one_k, 0)
+
+            @pl.when(qi == 0)
+            def _():
+                yown[h] = acc[...].T
+
+            for d in (1, 2):
+
+                @pl.when((qi == d) & helps[d])
+                def _():
+                    yout[d - 1, h] = acc[...].T.astype(jnp.bfloat16)
+                    y_copy(d, h).start()
+
+            return carry
+
+        return lax.fori_loop(0, n_q, one_q, carry)
+
+    lax.fori_loop(0, heads, forward, 0)
+
+    def norm(h, carry):
+        for d in (1, 2):
+
+            @pl.when(asks[d])
+            def _():
+                y_copy(d, h).wait_recv()
+                yown[h] = yown[h] + yin[d - 1, h].astype(jnp.float32)
+
+        y = yown[h]
+        centre = jnp.mean(y, -1, keepdims=True)
+        shifted = y - centre
+        inv_std = lax.rsqrt(jnp.mean(shifted * shifted, -1, keepdims=True) + 1e-05)
+        normed = shifted * inv_std
+        gate = proj[h, 0].astype(jnp.float32)
+        mixed[h] = (normed * gate).astype(jnp.bfloat16)
+        grad_mixed = cvec[...] * up[h].astype(jnp.float32)
+        grads[h, 0] = (grad_mixed * normed).astype(jnp.bfloat16)
+        grad_normed = grad_mixed * gate
+        grad_att = inv_std * (
+            grad_normed
+            - jnp.mean(grad_normed, -1, keepdims=True)
+            - normed * jnp.mean(grad_normed * normed, -1, keepdims=True)
+        )
+        gb[0, h] = grad_att.astype(jnp.bfloat16)
+        for d in (2, 1):
+
+            @pl.when(asks[d])
+            def _():
+                g_copy(d, h).start()
+
+        return carry
+
+    lax.fori_loop(0, heads, norm, 0)
+
+    def backward(h, carry):
+        dkv[...] = jnp.zeros_like(dkv)
+
+        def one_q(qi, carry):
+            for d in (1, 2):
+
+                @pl.when((qi == d) & helps[d])
+                def _():
+                    g_copy(d, h).wait_recv()
+
+            acc[...] = jnp.zeros_like(acc)
+            query = qb[qi, h]
+            grad = gb[qi, h]
+
+            def one_k(kj, carry):
+                pair = qi * 2 + kj
+                for t in range(2):
+                    part = pl.ds(t * half, half)
+                    dprod = dot(kb[kj, h, 1, part], grad, NT)
+                    edge = (dprod * stab[pair, h, part].astype(jnp.float32)).astype(jnp.bfloat16)
+                    acc[...] += dot(kb[kj, h, 0, part], edge, TN)
+                    dkv[kj, 0, part] += dot(edge, query, NN)
+                    dkv[kj, 1, part] += dot(ptab[pair, h, part], grad, NN)
+                return carry
+
+            lax.fori_loop(0, n_kv, one_k, 0)
+
+            @pl.when(qi == 0)
+            def _():
+                yown[h] = acc[...].T * scale
+
+            for d in (1, 2):
+
+                @pl.when((qi == d) & helps[d])
+                def _():
+                    dqout[d - 1, h] = (acc[...].T * scale).astype(jnp.bfloat16)
+                    dq_copy(d, h).start()
+
+            return carry
+
+        lax.fori_loop(0, n_q, one_q, 0)
+
+        @pl.when(me == 1)
+        def _():
+            dkvout[h, 0] = (dkv[1, 0] * scale).astype(jnp.bfloat16)
+            dkvout[h, 1] = dkv[1, 1].astype(jnp.bfloat16)
+            dkv_copy(h).start()
+
+        dkvown[h, 0] = dkv[0, 0] * scale
+        dkvown[h, 1] = dkv[0, 1]
+        return carry
+
+    lax.fori_loop(0, heads, backward, 0)
+
+    def finish(h, carry):
+        for d in (1, 2):
+
+            @pl.when(asks[d])
+            def _():
+                dq_copy(d, h).wait_recv()
+                yown[h] = yown[h] + dqin[d - 1, h].astype(jnp.float32)
+
+        @pl.when(me == 0)
+        def _():
+            dkv_copy(h).wait_recv()
+            dkvown[h] = dkvown[h] + dkvin[h].astype(jnp.float32)
+
+        grads[h, 1] = yown[h].astype(jnp.bfloat16)
+        grads[h, 2:4] = dkvown[h].astype(jnp.bfloat16)
+        return carry
+
+    lax.fori_loop(0, heads, finish, 0)
+
+    def drain(h, carry):
+        for d in (1, 2):
+
+            @pl.when(asks[d])
+            def _():
+                q_copy(d, h).wait_send()
+                g_copy(d, h).wait_send()
+
+            @pl.when(helps[d])
+            def _():
+                y_copy(d, h).wait_send()
+                dq_copy(d, h).wait_send()
+
+        @pl.when(me == 0)
+        def _():
+            kv_copy(h).wait_send()
+
+        @pl.when(me == 1)
+        def _():
+            dkv_copy(h).wait_send()
+
+        return carry
+
+    lax.fori_loop(0, heads, drain, 0)
+
+
+def four_shards(projected, upstream, ips_weight, item_ids, session_ids, session_blocks):
+    rows = projected[0]
+    count, heads, _, width = rows.shape
+    ctx_rank = lax.axis_index("ctx")
+    proj = jnp.transpose(rows, (1, 2, 0, 3))
+    up = jnp.transpose(upstream[0], (1, 0, 2))
+    weights_row = ips_weight[0]
+    items = item_ids[0]
+    fresh = jnp.concatenate(
+        [(items[1:] != items[:-1]).astype(jnp.float32), jnp.zeros((1,), jnp.float32)]
+    )
+    scaled = weights_row * fresh * weights_row.shape[0] / jnp.sum(weights_row)
+    cvec = lax.dynamic_slice_in_dim(scaled, ctx_rank * count, count)[:, None]
+    lists = session_blocks[0]
+    total = lists.shape[0]
+    listed = jnp.any(lists[:, :, None] == jnp.arange(total)[None, None, :], 1)
+    listed = jnp.broadcast_to(
+        listed.astype(jnp.float32).reshape(total * total, 1, 1), (total * total, 1, count)
+    )
+    sess_row = session_ids[0].reshape(total, 1, count)
+    sess_col = session_ids[0].reshape(total, count, 1)
+    bf, f32 = jnp.bfloat16, jnp.float32
+    vmem = pl.BlockSpec(memory_space=pltpu.VMEM)
+    piece = (heads, count, width)
+    sems = pltpu.SemaphoreType.DMA
+    mixed, grads = pl.pallas_call(
+        functools.partial(four_kernel, heads),
+        out_shape=(
+            jax.ShapeDtypeStruct(piece, bf),
+            jax.ShapeDtypeStruct((heads, 4, count, width), bf),
+        ),
+        in_specs=[vmem] * 6,
+        out_specs=(vmem, vmem),
+        scratch_shapes=[
+            pltpu.VMEM((3,) + piece, bf),
+            pltpu.VMEM((2, heads, 2, count, width), bf),
+            pltpu.VMEM((3,) + piece, bf),
+            pltpu.VMEM((2,) + piece, bf),
+            pltpu.VMEM((2,) + piece, bf),
+            pltpu.VMEM((2,) + piece, bf),
+            pltpu.VMEM((2,) + piece, bf),
+            pltpu.VMEM((heads, 2, count, width), bf),
+            pltpu.VMEM((heads, 2, count, width), bf),
+            pltpu.VMEM((6, heads, count, count), bf),
+            pltpu.VMEM((6, heads, count, count), bf),
+            pltpu.VMEM((6, count, count), f32),
+            pltpu.VMEM(piece, f32),
+            pltpu.VMEM((width, count), f32),
+            pltpu.VMEM((2, 2, count, width), f32),
+            pltpu.VMEM((heads, 2, count, width), f32),
+            sems((2, 2, heads)),
+            sems((2, 2, heads)),
+            sems((2, 2, heads)),
+            sems((2, 2, heads)),
+            sems((2, 1, heads)),
+            sems((2, 1, heads)),
+        ],
+        compiler_params=pltpu.CompilerParams(
+            collective_id=0, has_side_effects=True, vmem_limit_bytes=60 * 1024 * 1024
+        ),
+    )(proj, up, cvec, sess_row, sess_col, listed)
+    mixed = jnp.transpose(mixed, (1, 0, 2))
+    grads = jnp.transpose(grads, (2, 0, 1, 3))
+    return (mixed[None], grads[None])
+
+
 def solution(mesh):
+    body = four_shards if mesh.shape["ctx"] == 4 else shards
     placed = (
         P(("groups", "user"), "ctx", "head", None, None),
         P(("groups", "user"), "ctx", "head", None),
@@ -206,7 +582,7 @@
         P(("groups", "user"), None, None),
     )
     return jax.shard_map(
-        shards,
+        body,
         mesh=mesh,
         in_specs=placed,
         out_specs=(

time: 297 us -> 95.2 us (0.32)
  the two profiles are of different devices: /device:TPU:9 before, /device:TPU:0 now
where the time goes in v1:
time: 95.2 us; the launch traced here: 94.7 us
  Pallas kernels  73.6 us (77%)
  local copies, waits for them, and re-layouts  15.2 us (16%)
  other arithmetic  5.22 us (5%)
    pallas_call x1, Pallas kernels, four_shards(): pl.pallas_call(functools.partial(four_kernel, heads), out_shape=(jax.Shap...  73.6 us
    unnamed x7, local copies, waits for them, and re-layouts  11 us

profile of v1, /device:TPU:0, one launch (start us, length us, event | category | flops | bytes accessed | tf_op | source)
XLA Modules:
  0.0 94.7 jit_solution(7635477826761376986)
XLA Ops:
  0.6 0.0 copy-start
  0.6 1.5 %reduce_sum.9 = f32[]{:T(128)} reduce(f32[1,2048]{1,0:T(1,128)} %param.8, f32[]{:T(128)} %constant.5.clone.1), dimensions={0,1}, to_apply=%region_0.0 | reduce | flops 2047 | bytes 8200 | tf_op jit(solution)/shard_map/reduce_sum | solution.py:519
  2.1 0.9 compare_reduce_fusion
  3.0 1.4 %fusion.2 = f32[512]{0:T(512)S(1)} fusion(f32[2048]{0:T(1024)} %bitcast.28, s32[]{:T(128)S(6)} %select_n.3, pred[2047]{0:T(1024)(128)(4,1)S(1)} %compare_reduce_fusion, f32[]{:T(128)} %reduce_sum.9, pred[1]{0:T(512)(128)(4,1)} %constant.4.clone.1), kind=kLoop, calls=%fused_computation.8 | loop fusion | flops 2048 | bytes 6152 | tf_op jit(solution)/shard_map/div | solution.py:519
  4.4 0.7 copy.34
  5.1 0.1 fusion
  5.2 0.1 reshape.20
  5.3 0.5 broadcast.11
  5.8 1.4 %reduce.6 = s32[2048]{0:T(1024)S(1)} reduce(s32[1,2048]{1,0:T(1,128)} %param.10, s32[]{:T(128)} %broadcast.11), dimensions={0}, to_apply=%param.10.reduce_sub_computation.3 | reduce | bytes 16388 | tf_op args[4]
  7.2 0.7 broadcast_in_dim.16.listed
  7.8 0.9 copy.24.cvec
  8.7 1.9 %copy.33 = bf16[1,512,4,128]{3,1,2,0:T(8,128)(2,1)} copy(bf16[1,512,4,128]{3,2,1,0:T(4,128)(2,1)} %param.7) | data formatting | bytes 1048576 | tf_op args[1]
  10.6 1.9 %reshape_squeeze.8.sess_col = s32[4,512,1]{2,1,0:T(8,128)} reshape(s32[2048]{0:T(1024)S(1)} %reduce.6) | data formatting | bytes 16384 | tf_op jit(solution)/shard_map/reshape;squeeze | solution.py:528
  12.5 0.0 copy-done
  12.5 1.9 %copy.32 = bf16[1,512,4,4,128]{4,1,3,2,0:T(8,128)(2,1)} copy(bf16[1,512,4,4,128]{4,3,2,1,0:T(4,128)(2,1)S(1)} %copy-done) | data formatting | bytes 4194304 | tf_op args[0]
  14.3 73.6 %shard_map.77 = (bf16[4,512,128]{2,1,0:T(8,128)(2,1)}, bf16[4,4,512,128]{3,2,1,0:T(8,128)(2,1)}) custom-call(bf16[4,4,512,128]{3,2,1,0:T(8,128)(2,1)} %bitcast.23, bf16[4,512,128]{2,1,0:T(8,128)(2,1)} %bitcast.24, f32[512,1]{1,0:T(8,128)} %copy.24.cvec, s32[4,1,512]{2,1,0:T(1,128)} %bitcast.27, s32[4,512,1]{2,1,0:T(8,128)} %reshape_squeeze.8.sess_col, ...), custom_call_target="tpu_custom_call" | custom-call | tf_op jit(solution)/shard_map/pallas_call | solution.py:533
  87.9 2.2 %copy.26 = bf16[1,512,4,128]{3,2,1,0:T(4,128)(2,1)} copy(bf16[1,512,4,128]{3,1,2,0:T(8,128)(2,1)} %bitcast.26) | data formatting | bytes 1048576
  90.2 4.5 %copy.27 = bf16[1,512,4,4,128]{4,3,2,1,0:T(4,128)(2,1)} copy(bf16[1,512,4,4,128]{4,1,3,2,0:T(8,128)(2,1)} %bitcast.25) | data formatting | bytes 4194304
  (1 shorter events, 0.0 us)
Async XLA Ops:
  0.6 11.8 %copy-start = (bf16[1,512,4,4,128]{4,3,2,1,0:T(4,128)(2,1)S(1)}, bf16[1,512,4,4,128]{4,3,2,1,0:T(4,128)(2,1)}, u32[]{:S(2)}) copy-start(bf16[1,512,4,4,128]{4,3,2,1,0:T(4,128)(2,1)} %param.6) | copy-start | bytes 6291460

commit v2 on v1

--- a/solution.py
+++ b/solution.py
@@ -213,10 +213,10 @@
     heads,
     proj,
     up,
-    cvec,
-    sess_row,
-    sess_col,
-    listed,
+    weights,
+    items,
+    sessions,
+    lists,
     mixed,
     grads,
     qb,
@@ -235,6 +235,8 @@
     acc,
     dkv,
     dkvown,
+    rowbuf,
+    cmat,
     q_sem,
     y_sem,
     g_sem,
@@ -244,10 +246,34 @@
 ):
     me = lax.axis_index("ctx")
     block, width = up.shape[1], up.shape[2]
+    total = weights.shape[1]
     scale = width ** (-0.5)
-    half = block // 2
-    n_q = jnp.where(me == 1, 3, jnp.where(me == 2, 2, 1))
-    n_kv = jnp.where(me == 1, 2, 1)
+    chunks = 2
+    step = block // chunks
+
+    def odd(h):
+        return lax.rem(jnp.int32(h), jnp.int32(2)) == 1
+
+    def n_q(h):
+        return jnp.where(me == 2, 2, jnp.where((me == 1) & jnp.logical_not(odd(h)), 3, 1))
+
+    def n_kv(h):
+        return jnp.where(me == 1, 2, jnp.where((me == 2) & odd(h), 3, 1))
+
+    def helps(d, h):
+        return n_q(h) > d
+
+    def asks(d, h):
+        return jnp.where(odd(h), me == 3 if d == 1 else me > 3, me >= d + 1)
+
+    def takes(d, h):
+        return n_kv(h) > d
+
+    def gives(d, h):
+        return jnp.where(odd(h), me <= 2 - d, me == 0 if d == 1 else me < 0)
+
+    max_q = jnp.where(me == 1, 3, jnp.where(me == 2, 2, 1))
+    max_kv = jnp.where(me == 1, 2, jnp.where(me == 2, 3, 1))
 
     barrier = pltpu.get_barrier_semaphore()
     for d in range(1, 4):
@@ -278,60 +304,74 @@
     def dq_copy(d, h):
         return remote(dqout.at[d - 1, h], dqin.at[d - 1, h], dq_sem, d - 1, h, lax.rem(me + d, 4))
 
-    def kv_copy(h):
-        return remote(proj.at[h, pl.ds(2, 2)], kb.at[1, h], kv_sem, 0, h, lax.rem(me + 1, 4))
-
-    def dkv_copy(h):
-        return remote(dkvout.at[h], dkvin.at[h], dkv_sem, 0, h, lax.rem(me + 3, 4))
-
-    asks = {1: me >= 2, 2: me == 3}
-    helps = {1: (me == 1) | (me == 2), 2: me == 1}
+    def kv_copy(d, h):
+        return remote(
+            proj.at[h, pl.ds(2, 2)], kb.at[d, h], kv_sem, d - 1, h, lax.rem(me + d, 4)
+        )
+
+    def dkv_copy(d, h):
+        return remote(
+            dkvout.at[d - 1, h], dkvin.at[d - 1, h], dkv_sem, d - 1, h, lax.rem(me + 4 - d, 4)
+        )
 
     for h in range(heads):
         for d in (2, 1):
 
-            @pl.when(asks[d])
+            @pl.when(asks(d, h))
             def _():
                 q_copy(d, h).start()
 
-        @pl.when(me == 0)
-        def _():
-            kv_copy(h).start()
+            @pl.when(gives(d, h))
+            def _():
+                kv_copy(d, h).start()
 
     qb[0] = proj[:, 1]
     kb[0] = proj[:, 2:4]
 
+    def run_row(source, index):
+        rowbuf[0:1] = source
+        return rowbuf[0:1, pl.ds(pl.multiple_of(index * block, block), block)]
+
+    def down(row):
+        return jnp.broadcast_to(row, (width, block)).T
+
+    ids = items[...]
+    place = lax.broadcasted_iota(jnp.int32, (1, total), 1)
+    fresh = (pltpu.roll(ids, total - 1, 1) != ids) & (place < total - 1)
+    loss = weights[...]
+    loss = loss * jnp.where(fresh, 1.0, 0.0) * total / jnp.sum(loss)
+    cmat[...] = down(run_row(loss, me))
+
     def fill(pair, carry):
-        qi, kj = pair // 2, lax.rem(pair, 2)
-
-        @pl.when((qi < n_q) & (kj < n_kv))
-        def _():
-            bq, bk = me + qi, me - kj
-            row = sess_row[bq]
-            gap = bq - bk
-            full = listed[bq * 4 + bk]
-            for t in range(2):
-                col = sess_col[bk, pl.ds(t * half, half)]
-                c = lax.broadcasted_iota(jnp.int32, (half, block), 0) + t * half
-                a = lax.broadcasted_iota(jnp.int32, (half, block), 1)
-                ahead = a - c + gap * block
-                window = (ahead >= 0) & (ahead < block)
-                near = jnp.where(window & (row == col), 1.0, 0.0)
-                mask[pair, pl.ds(t * half, half)] = jnp.maximum(near, full)
-
+        qi, kj = pair // max_kv, lax.rem(pair, max_kv)
+        bq, bk = me + qi, me - kj
+        row = run_row(sessions[...].astype(jnp.float32), bq)
+        col = down(run_row(sessions[...].astype(jnp.float32), bk))
+        col = jnp.concatenate([col] * (block // width), 1)
+        full = jnp.float32(0.0)
+        for slot in range(lists.shape[0]):
+            full = jnp.maximum(full, jnp.where(lists[slot, 0, bq] == bk, 1.0, 0.0))
+        c = lax.broadcasted_iota(jnp.int32, (block, block), 0)
+        a = lax.broadcasted_iota(jnp.int32, (block, block), 1)
+        ahead = a - c + (bq - bk) * block
+        window = (ahead >= 0) & (ahead < block)
+        near = jnp.where(window & (row == col), 1.0, 0.0)
+        mask[pair] = jnp.maximum(near, full).astype(jnp.bfloat16)
         return carry
 
-    lax.fori_loop(0, 6, fill, 0)
+    lax.fori_loop(0, max_q * max_kv, fill, 0)
 
     def forward(h, carry):
-        @pl.when(me == 1)
-        def _():
-            kv_copy(h).wait_recv()
+        for d in (1, 2):
+
+            @pl.when(takes(d, h))
+            def _():
+                kv_copy(d, h).wait_recv()
 
         def one_q(qi, carry):
             for d in (1, 2):
 
-                @pl.when((qi == d) & helps[d])
+                @pl.when((qi == d) & helps(d, h))
                 def _():
                     q_copy(d, h).wait_recv()
 
@@ -339,21 +379,21 @@
             query = qb[qi, h]
 
             def one_k(kj, carry):
-                pair = qi * 2 + kj
-                for t in range(2):
-                    part = pl.ds(t * half, half)
+                pair = qi * n_kv(h) + kj
+                for t in range(chunks):
+                    part = pl.ds(t * step, step)
                     raw = dot(kb[kj, h, 0, part], query, NT)
                     sigma = 0.5 * jnp.tanh(raw * (0.5 * scale)) + 0.5
                     prob = raw * scale * sigma
                     slope = sigma + prob * (1.0 - sigma)
-                    seen = mask[pair, part]
-                    prob = (prob * seen).astype(jnp.bfloat16)
+                    seen = mask[qi * max_kv + kj, part]
+                    prob = prob.astype(jnp.bfloat16) * seen
                     ptab[pair, h, part] = prob
-                    stab[pair, h, part] = (slope * seen).astype(jnp.bfloat16)
+                    stab[pair, h, part] = slope.astype(jnp.bfloat16) * seen
                     acc[...] += dot(kb[kj, h, 1, part], prob, TN)
                 return carry
 
-            lax.fori_loop(0, n_kv, one_k, 0)
+            lax.fori_loop(0, n_kv(h), one_k, 0)
 
             @pl.when(qi == 0)
             def _():
@@ -361,21 +401,21 @@
 
             for d in (1, 2):
 
-                @pl.when((qi == d) & helps[d])
+                @pl.when((qi == d) & helps(d, h))
                 def _():
                     yout[d - 1, h] = acc[...].T.astype(jnp.bfloat16)
                     y_copy(d, h).start()
 
             return carry
 
-        return lax.fori_loop(0, n_q, one_q, carry)
+        return lax.fori_loop(0, n_q(h), one_q, carry)
 
     lax.fori_loop(0, heads, forward, 0)
 
     def norm(h, carry):
         for d in (1, 2):
 
-            @pl.when(asks[d])
+            @pl.when(asks(d, h))
             def _():
                 y_copy(d, h).wait_recv()
                 yown[h] = yown[h] + yin[d - 1, h].astype(jnp.float32)
@@ -387,7 +427,7 @@
         normed = shifted * inv_std
         gate = proj[h, 0].astype(jnp.float32)
         mixed[h] = (normed * gate).astype(jnp.bfloat16)
-        grad_mixed = cvec[...] * up[h].astype(jnp.float32)
+        grad_mixed = cmat[...] * up[h].astype(jnp.float32)
         grads[h, 0] = (grad_mixed * normed).astype(jnp.bfloat16)
         grad_normed = grad_mixed * gate
         grad_att = inv_std * (
@@ -398,7 +438,7 @@
         gb[0, h] = grad_att.astype(jnp.bfloat16)
         for d in (2, 1):
 
-            @pl.when(asks[d])
+            @pl.when(asks(d, h))
             def _():
                 g_copy(d, h).start()
 
@@ -412,7 +452,7 @@
         def one_q(qi, carry):
             for d in (1, 2):
 
-                @pl.when((qi == d) & helps[d])
+                @pl.when((qi == d) & helps(d, h))
                 def _():
                     g_copy(d, h).wait_recv()
 
@@ -421,9 +461,9 @@
             grad = gb[qi, h]
 
             def one_k(kj, carry):
-                pair = qi * 2 + kj
-                for t in range(2):
-                    part = pl.ds(t * half, half)
+                pair = qi * n_kv(h) + kj
+                for t in range(chunks):
+                    part = pl.ds(t * step, step)
                     dprod = dot(kb[kj, h, 1, part], grad, NT)
                     edge = (dprod * stab[pair, h, part].astype(jnp.float32)).astype(jnp.bfloat16)
                     acc[...] += dot(kb[kj, h, 0, part], edge, TN)
@@ -431,7 +471,7 @@
                     dkv[kj, 1, part] += dot(ptab[pair, h, part], grad, NN)
                 return carry
 
-            lax.fori_loop(0, n_kv, one_k, 0)
+            lax.fori_loop(0, n_kv(h), one_k, 0)
 
             @pl.when(qi == 0)
             def _():
@@ -439,20 +479,22 @@
 
             for d in (1, 2):
 
-                @pl.when((qi == d) & helps[d])
+                @pl.when((qi == d) & helps(d, h))
                 def _():
                     dqout[d - 1, h] = (acc[...].T * scale).astype(jnp.bfloat16)
                     dq_copy(d, h).start()
 
             return carry
 
-        lax.fori_loop(0, n_q, one_q, 0)
-
-        @pl.when(me == 1)
-        def _():
-            dkvout[h, 0] = (dkv[1, 0] * scale).astype(jnp.bfloat16)
-            dkvout[h, 1] = dkv[1, 1].astype(jnp.bfloat16)
-            dkv_copy(h).start()
+        lax.fori_loop(0, n_q(h), one_q, 0)
+
+        for d in (2, 1):
+
+            @pl.when(takes(d, h))
+            def _():
+                dkvout[d - 1, h, 0] = (dkv[d, 0] * scale).astype(jnp.bfloat16)
+                dkvout[d - 1, h, 1] = dkv[d, 1].astype(jnp.bfloat16)
+                dkv_copy(d, h).start()
 
         dkvown[h, 0] = dkv[0, 0] * scale
         dkvown[h, 1] = dkv[0, 1]
@@ -463,15 +505,15 @@
     def finish(h, carry):
         for d in (1, 2):
 
-            @pl.when(asks[d])
+            @pl.when(asks(d, h))
             def _():
                 dq_copy(d, h).wait_recv()
                 yown[h] = yown[h] + dqin[d - 1, h].astype(jnp.float32)
 
-        @pl.when(me == 0)
-        def _():
-            dkv_copy(h).wait_recv()
-            dkvown[h] = dkvown[h] + dkvin[h].astype(jnp.float32)
+            @pl.when(gives(d, h))
+            def _():
+                dkv_copy(d, h).wait_recv()
+                dkvown[h] = dkvown[h] + dkvin[d - 1, h].astype(jnp.float32)
 
         grads[h, 1] = yown[h].astype(jnp.bfloat16)
         grads[h, 2:4] = dkvown[h].astype(jnp.bfloat16)
@@ -482,23 +524,23 @@
     def drain(h, carry):
         for d in (1, 2):
 
-            @pl.when(asks[d])
+            @pl.when(asks(d, h))
             def _():
                 q_copy(d, h).wait_send()
                 g_copy(d, h).wait_send()
 
-            @pl.when(helps[d])
+            @pl.when(helps(d, h))
             def _():
                 y_copy(d, h).wait_send()
                 dq_copy(d, h).wait_send()
 
-        @pl.when(me == 0)
-        def _():
-            kv_copy(h).wait_send()
-
-        @pl.when(me == 1)
-        def _():
-            dkv_copy(h).wait_send()
+            @pl.when(gives(d, h))
+            def _():
+                kv_copy(d, h).wait_send()
+
+            @pl.when(takes(d, h))
+            def _():
+                dkv_copy(d, h).wait_send()
 
         return carry
 
@@ -508,24 +550,9 @@
 def four_shards(projected, upstream, ips_weight, item_ids, session_ids, session_blocks):
     rows = projected[0]
     count, heads, _, width = rows.shape
-    ctx_rank = lax.axis_index("ctx")
     proj = jnp.transpose(rows, (1, 2, 0, 3))
     up = jnp.transpose(upstream[0], (1, 0, 2))
-    weights_row = ips_weight[0]
-    items = item_ids[0]
-    fresh = jnp.concatenate(
-        [(items[1:] != items[:-1]).astype(jnp.float32), jnp.zeros((1,), jnp.float32)]
-    )
-    scaled = weights_row * fresh * weights_row.shape[0] / jnp.sum(weights_row)
-    cvec = lax.dynamic_slice_in_dim(scaled, ctx_rank * count, count)[:, None]
-    lists = session_blocks[0]
-    total = lists.shape[0]
-    listed = jnp.any(lists[:, :, None] == jnp.arange(total)[None, None, :], 1)
-    listed = jnp.broadcast_to(
-        listed.astype(jnp.float32).reshape(total * total, 1, 1), (total * total, 1, count)
-    )
-    sess_row = session_ids[0].reshape(total, 1, count)
-    sess_col = session_ids[0].reshape(total, count, 1)
+    lists = jnp.transpose(session_blocks, (2, 0, 1))
     bf, f32 = jnp.bfloat16, jnp.float32
     vmem = pl.BlockSpec(memory_space=pltpu.VMEM)
     piece = (heads, count, width)
@@ -536,36 +563,38 @@
             jax.ShapeDtypeStruct(piece, bf),
             jax.ShapeDtypeStruct((heads, 4, count, width), bf),
         ),
-        in_specs=[vmem] * 6,
+        in_specs=[vmem] * 5 + [pl.BlockSpec(memory_space=pltpu.SMEM)],
         out_specs=(vmem, vmem),
         scratch_shapes=[
             pltpu.VMEM((3,) + piece, bf),
-            pltpu.VMEM((2, heads, 2, count, width), bf),
+            pltpu.VMEM((3, heads, 2, count, width), bf),
             pltpu.VMEM((3,) + piece, bf),
             pltpu.VMEM((2,) + piece, bf),
             pltpu.VMEM((2,) + piece, bf),
             pltpu.VMEM((2,) + piece, bf),
             pltpu.VMEM((2,) + piece, bf),
-            pltpu.VMEM((heads, 2, count, width), bf),
-            pltpu.VMEM((heads, 2, count, width), bf),
+            pltpu.VMEM((2, heads, 2, count, width), bf),
+            pltpu.VMEM((2, heads, 2, count, width), bf),
             pltpu.VMEM((6, heads, count, count), bf),
             pltpu.VMEM((6, heads, count, count), bf),
-            pltpu.VMEM((6, count, count), f32),
+            pltpu.VMEM((6, count, count), bf),
             pltpu.VMEM(piece, f32),
             pltpu.VMEM((width, count), f32),
-            pltpu.VMEM((2, 2, count, width), f32),
+            pltpu.VMEM((3, 2, count, width), f32),
             pltpu.VMEM((heads, 2, count, width), f32),
+            pltpu.VMEM((8, ips_weight.shape[1]), f32),
+            pltpu.VMEM((count, width), f32),
             sems((2, 2, heads)),
             sems((2, 2, heads)),
             sems((2, 2, heads)),
             sems((2, 2, heads)),
-            sems((2, 1, heads)),
-            sems((2, 1, heads)),
+            sems((2, 2, heads)),
+            sems((2, 2, heads)),
         ],
         compiler_params=pltpu.CompilerParams(
             collective_id=0, has_side_effects=True, vmem_limit_bytes=60 * 1024 * 1024
         ),
-    )(proj, up, cvec, sess_row, sess_col, listed)
+    )(proj, up, ips_weight, item_ids, session_ids, lists)
     mixed = jnp.transpose(mixed, (1, 0, 2))
     grads = jnp.transpose(grads, (2, 0, 1, 3))
     return (mixed[None], grads[None])

time: 95.2 us -> 102 us (1.071)
  Pallas kernels: 73.6 us -> 89.1 us
  other arithmetic: 5.22 us -> 0 us
  local copies, waits for them, and re-layouts: 15.2 us -> 12.1 us
    pallas_call x1, Pallas kernels: 73.6 us -> 89.1 us  [four_shards(): pl.pallas_call(functools.partial(four_kernel, heads), out_shape=(jax.Shap...]
    another operation x1 -> x0, local copies, waits for them, and re-layouts: 1.86 us -> none  [four_shards(): sess_col = session_ids[0].reshape(total, count, 1)]
    broadcast_in_dim x2 -> x0, local copies, waits for them, and re-layouts: 1.54 us -> none  [the longest x1 0.85 us: four_shards(): cvec = lax.dynamic_slice_in_dim(scaled, ctx_rank * count, count)[:, None]]
    reduce_sum x1 -> x0, other arithmetic: 1.47 us -> none  [four_shards(): scaled = weights_row * fresh * weights_row.shape[0] / jnp.sum(weights_row)]
    div x1 -> x0, other arithmetic: 1.42 us -> none  [four_shards(): scaled = weights_row * fresh * weights_row.shape[0] / jnp.sum(weights_row)]
    unnamed x1 -> x0, other arithmetic: 1.36 us -> none
    unnamed x7 -> x4, local copies, waits for them, and re-layouts: 11 us -> 12.1 us
where the time goes in v2:
time: 102 us
  Pallas kernels  89.1 us (87%)
  local copies, waits for them, and re-layouts  12.1 us (12%)
    pallas_call x1, Pallas kernels, four_shards(): pl.pallas_call(functools.partial(four_kernel, heads), out_shape=(jax.Shap...  89.1 us
    unnamed x4, local copies, waits for them, and re-layouts  12.1 us

profile of v2, /device:TPU:0, one launch (start us, length us, event | category | flops | bytes accessed | tf_op | source)
XLA Modules:
  0.0 101.8 jit_solution(9830103262462694970)
XLA Ops:
  0.6 1.9 %copy.15 = bf16[1,512,4,128]{3,1,2,0:T(8,128)(2,1)} copy(bf16[1,512,4,128]{3,2,1,0:T(4,128)(2,1)} %param.7) | data formatting | bytes 1048576 | tf_op args[1]
  2.5 3.5 %copy.14 = bf16[1,512,4,4,128]{4,1,3,2,0:T(8,128)(2,1)} copy(bf16[1,512,4,4,128]{4,3,2,1,0:T(4,128)(2,1)} %param.6) | data formatting | bytes 4194304 | tf_op args[0]
  6.0 89.1 %shard_map.77 = (bf16[4,512,128]{2,1,0:T(8,128)(2,1)}, bf16[4,4,512,128]{3,2,1,0:T(8,128)(2,1)}) custom-call(bf16[4,4,512,128]{3,2,1,0:T(8,128)(2,1)} %bitcast.17, bf16[4,512,128]{2,1,0:T(8,128)(2,1)} %bitcast.19, f32[1,2048]{1,0:T(1,128)} %weights.1, s32[1,2048]{1,0:T(1,128)} %items.1, s32[1,2048]{1,0:T(1,128)} %sessions.1, s32[3,1,4]{2,1,0:T(1,128)} %bitcast.21), custom_call_target="tpu_custom_call" | custom-call | tf_op jit(solution)/shard_map/pallas_call | solution.py:560
  95.1 2.2 %copy.10 = bf16[1,512,4,128]{3,2,1,0:T(4,128)(2,1)} copy(bf16[1,512,4,128]{3,1,2,0:T(8,128)(2,1)} %bitcast.20) | data formatting | bytes 1048576
  97.3 4.5 %copy.11 = bf16[1,512,4,4,128]{4,3,2,1,0:T(4,128)(2,1)} copy(bf16[1,512,4,4,128]{4,1,3,2,0:T(8,128)(2,1)} %bitcast.18) | data formatting | bytes 4194304

commit v3 on v1

--- a/solution.py
+++ b/solution.py
@@ -213,10 +213,10 @@
     heads,
     proj,
     up,
-    cvec,
-    sess_row,
-    sess_col,
-    listed,
+    weights,
+    items,
+    sessions,
+    lists,
     mixed,
     grads,
     qb,
@@ -235,6 +235,9 @@
     acc,
     dkv,
     dkvown,
+    rowbuf,
+    cmat,
+    edges,
     q_sem,
     y_sem,
     g_sem,
@@ -244,10 +247,18 @@
 ):
     me = lax.axis_index("ctx")
     block, width = up.shape[1], up.shape[2]
+    total = weights.shape[1]
     scale = width ** (-0.5)
-    half = block // 2
-    n_q = jnp.where(me == 1, 3, jnp.where(me == 2, 2, 1))
-    n_kv = jnp.where(me == 1, 2, 1)
+    chunks = 2
+    step = block // chunks
+
+    n_q = jnp.where(me == 1, 3, jnp.where(me == 3, 1, 2))
+
+    def n_kv(qi):
+        return jnp.where((me == 1) & (qi > 0), 2, 1)
+
+    asks = {1: me >= 1, 2: me == 3}
+    helps = {1: me <= 2, 2: me == 1}
 
     barrier = pltpu.get_barrier_semaphore()
     for d in range(1, 4):
@@ -279,13 +290,14 @@
         return remote(dqout.at[d - 1, h], dqin.at[d - 1, h], dq_sem, d - 1, h, lax.rem(me + d, 4))
 
     def kv_copy(h):
-        return remote(proj.at[h, pl.ds(2, 2)], kb.at[1, h], kv_sem, 0, h, lax.rem(me + 1, 4))
+        return remote(
+            proj.at[h, pl.ds(2, 2)], kb.at[1, h], kv_sem, 0, h, lax.rem(me + 1, 4)
+        )
 
     def dkv_copy(h):
-        return remote(dkvout.at[h], dkvin.at[h], dkv_sem, 0, h, lax.rem(me + 3, 4))
-
-    asks = {1: me >= 2, 2: me == 3}
-    helps = {1: (me == 1) | (me == 2), 2: me == 1}
+        return remote(
+            dkvout.at[h], dkvin.at[h], dkv_sem, 0, h, lax.rem(me + 3, 4)
+        )
 
     for h in range(heads):
         for d in (2, 1):
@@ -301,34 +313,51 @@
     qb[0] = proj[:, 1]
     kb[0] = proj[:, 2:4]
 
+    def run_row(source, index):
+        rowbuf[0:1] = source
+        return rowbuf[0:1, pl.ds(pl.multiple_of(index * block, block), block)]
+
+    def down(row):
+        return jnp.broadcast_to(row, (width, block)).T
+
+    ids = items[...]
+    place = lax.broadcasted_iota(jnp.int32, (1, total), 1)
+    fresh = (pltpu.roll(ids, total - 1, 1) != ids) & (place < total - 1)
+    loss = weights[...]
+    loss = loss * jnp.where(fresh, 1.0, 0.0) * total / jnp.sum(loss)
+    cmat[...] = down(run_row(loss, me))
+
     def fill(pair, carry):
         qi, kj = pair // 2, lax.rem(pair, 2)
 
-        @pl.when((qi < n_q) & (kj < n_kv))
+        @pl.when((qi < n_q) & (kj < n_kv(qi)))
         def _():
-            bq, bk = me + qi, me - kj
-            row = sess_row[bq]
-            gap = bq - bk
-            full = listed[bq * 4 + bk]
-            for t in range(2):
-                col = sess_col[bk, pl.ds(t * half, half)]
-                c = lax.broadcasted_iota(jnp.int32, (half, block), 0) + t * half
-                a = lax.broadcasted_iota(jnp.int32, (half, block), 1)
-                ahead = a - c + gap * block
-                window = (ahead >= 0) & (ahead < block)
-                near = jnp.where(window & (row == col), 1.0, 0.0)
-                mask[pair, pl.ds(t * half, half)] = jnp.maximum(near, full)
+            fill_one(pair, me + qi, me - kj)
 
         return carry
 
+    def fill_one(pair, bq, bk):
+        row = run_row(sessions[...].astype(jnp.float32), bq)
+        col = down(run_row(sessions[...].astype(jnp.float32), bk))
+        col = jnp.concatenate([col] * (block // width), 1)
+        full = jnp.float32(0.0)
+        for slot in range(lists.shape[0]):
+            full = jnp.maximum(full, jnp.where(lists[slot, 0, bq] == bk, 1.0, 0.0))
+        c = lax.broadcasted_iota(jnp.int32, (block, block), 0)
+        a = lax.broadcasted_iota(jnp.int32, (block, block), 1)
+        ahead = a - c + (bq - bk) * block
+        window = (ahead >= 0) & (ahead < block)
+        near = jnp.where(window & (row == col), 1.0, 0.0)
+        mask[pair] = jnp.maximum(near, full).astype(jnp.bfloat16)
+
     lax.fori_loop(0, 6, fill, 0)
 
     def forward(h, carry):
-        @pl.when(me == 1)
-        def _():
-            kv_copy(h).wait_recv()
-
         def one_q(qi, carry):
+            @pl.when((qi == 1) & (me == 1))
+            def _():
+                kv_copy(h).wait_recv()
+
             for d in (1, 2):
 
                 @pl.when((qi == d) & helps[d])
@@ -340,20 +369,20 @@
 
             def one_k(kj, carry):
                 pair = qi * 2 + kj
-                for t in range(2):
-                    part = pl.ds(t * half, half)
+                for t in range(chunks):
+                    part = pl.ds(t * step, step)
                     raw = dot(kb[kj, h, 0, part], query, NT)
                     sigma = 0.5 * jnp.tanh(raw * (0.5 * scale)) + 0.5
                     prob = raw * scale * sigma
                     slope = sigma + prob * (1.0 - sigma)
                     seen = mask[pair, part]
-                    prob = (prob * seen).astype(jnp.bfloat16)
+                    prob = prob.astype(jnp.bfloat16) * seen
                     ptab[pair, h, part] = prob
-                    stab[pair, h, part] = (slope * seen).astype(jnp.bfloat16)
-                    acc[...] += dot(kb[kj, h, 1, part], prob, TN)
+                    stab[pair, h, part] = slope.astype(jnp.bfloat16) * seen
+                acc[...] += dot(kb[kj, h, 1], ptab[pair, h], TN)
                 return carry
 
-            lax.fori_loop(0, n_kv, one_k, 0)
+            lax.fori_loop(0, n_kv(qi), one_k, 0)
 
             @pl.when(qi == 0)
             def _():
@@ -387,7 +416,7 @@
         normed = shifted * inv_std
         gate = proj[h, 0].astype(jnp.float32)
         mixed[h] = (normed * gate).astype(jnp.bfloat16)
-        grad_mixed = cvec[...] * up[h].astype(jnp.float32)
+        grad_mixed = cmat[...] * up[h].astype(jnp.float32)
         grads[h, 0] = (grad_mixed * normed).astype(jnp.bfloat16)
         grad_normed = grad_mixed * gate
         grad_att = inv_std * (
@@ -422,16 +451,17 @@
 
             def one_k(kj, carry):
                 pair = qi * 2 + kj
-                for t in range(2):
-                    part = pl.ds(t * half, half)
+                for t in range(chunks):
+                    part = pl.ds(t * step, step)
                     dprod = dot(kb[kj, h, 1, part], grad, NT)
                     edge = (dprod * stab[pair, h, part].astype(jnp.float32)).astype(jnp.bfloat16)
-                    acc[...] += dot(kb[kj, h, 0, part], edge, TN)
+                    edges[part] = edge
                     dkv[kj, 0, part] += dot(edge, query, NN)
                     dkv[kj, 1, part] += dot(ptab[pair, h, part], grad, NN)
+                acc[...] += dot(kb[kj, h, 0], edges[...], TN)
                 return carry
 
-            lax.fori_loop(0, n_kv, one_k, 0)
+            lax.fori_loop(0, n_kv(qi), one_k, 0)
 
             @pl.when(qi == 0)
             def _():
@@ -508,24 +538,9 @@
 def four_shards(projected, upstream, ips_weight, item_ids, session_ids, session_blocks):
     rows = projected[0]
     count, heads, _, width = rows.shape
-    ctx_rank = lax.axis_index("ctx")
     proj = jnp.transpose(rows, (1, 2, 0, 3))
     up = jnp.transpose(upstream[0], (1, 0, 2))
-    weights_row = ips_weight[0]
-    items = item_ids[0]
-    fresh = jnp.concatenate(
-        [(items[1:] != items[:-1]).astype(jnp.float32), jnp.zeros((1,), jnp.float32)]
-    )
-    scaled = weights_row * fresh * weights_row.shape[0] / jnp.sum(weights_row)
-    cvec = lax.dynamic_slice_in_dim(scaled, ctx_rank * count, count)[:, None]
-    lists = session_blocks[0]
-    total = lists.shape[0]
-    listed = jnp.any(lists[:, :, None] == jnp.arange(total)[None, None, :], 1)
-    listed = jnp.broadcast_to(
-        listed.astype(jnp.float32).reshape(total * total, 1, 1), (total * total, 1, count)
-    )
-    sess_row = session_ids[0].reshape(total, 1, count)
-    sess_col = session_ids[0].reshape(total, count, 1)
+    lists = jnp.transpose(session_blocks, (2, 0, 1))
     bf, f32 = jnp.bfloat16, jnp.float32
     vmem = pl.BlockSpec(memory_space=pltpu.VMEM)
     piece = (heads, count, width)
@@ -536,7 +551,7 @@
             jax.ShapeDtypeStruct(piece, bf),
             jax.ShapeDtypeStruct((heads, 4, count, width), bf),
         ),
-        in_specs=[vmem] * 6,
+        in_specs=[vmem] * 5 + [pl.BlockSpec(memory_space=pltpu.SMEM)],
         out_specs=(vmem, vmem),
         scratch_shapes=[
             pltpu.VMEM((3,) + piece, bf),
@@ -550,11 +565,14 @@
             pltpu.VMEM((heads, 2, count, width), bf),
             pltpu.VMEM((6, heads, count, count), bf),
             pltpu.VMEM((6, heads, count, count), bf),
-            pltpu.VMEM((6, count, count), f32),
+            pltpu.VMEM((6, count, count), bf),
             pltpu.VMEM(piece, f32),
             pltpu.VMEM((width, count), f32),
             pltpu.VMEM((2, 2, count, width), f32),
             pltpu.VMEM((heads, 2, count, width), f32),
+            pltpu.VMEM((8, ips_weight.shape[1]), f32),
+            pltpu.VMEM((count, width), f32),
+            pltpu.VMEM((count, count), bf),
             sems((2, 2, heads)),
             sems((2, 2, heads)),
             sems((2, 2, heads)),
@@ -565,7 +583,7 @@
         compiler_params=pltpu.CompilerParams(
             collective_id=0, has_side_effects=True, vmem_limit_bytes=60 * 1024 * 1024
         ),
-    )(proj, up, cvec, sess_row, sess_col, listed)
+    )(proj, up, ips_weight, item_ids, session_ids, lists)
     mixed = jnp.transpose(mixed, (1, 0, 2))
     grads = jnp.transpose(grads, (2, 0, 1, 3))
     return (mixed[None], grads[None])

time: 95.2 us -> 85.7 us (0.900)
  other arithmetic: 5.22 us -> 0 us
  local copies, waits for them, and re-layouts: 15.2 us -> 12.1 us
  Pallas kernels: 73.6 us -> 72.6 us
    another operation x1 -> x0, local copies, waits for them, and re-layouts: 1.86 us -> none  [four_shards(): sess_col = session_ids[0].reshape(total, count, 1)]
    broadcast_in_dim x2 -> x0, local copies, waits for them, and re-layouts: 1.54 us -> none  [the longest x1 0.85 us: four_shards(): cvec = lax.dynamic_slice_in_dim(scaled, ctx_rank * count, count)[:, None]]
    reduce_sum x1 -> x0, other arithmetic: 1.47 us -> none  [four_shards(): scaled = weights_row * fresh * weights_row.shape[0] / jnp.sum(weights_row)]
    div x1 -> x0, other arithmetic: 1.42 us -> none  [four_shards(): scaled = weights_row * fresh * weights_row.shape[0] / jnp.sum(weights_row)]
    unnamed x1 -> x0, other arithmetic: 1.36 us -> none
    unnamed x7 -> x4, local copies, waits for them, and re-layouts: 11 us -> 12.1 us
    pallas_call x1, Pallas kernels: 73.6 us -> 72.6 us  [four_shards(): pl.pallas_call(functools.partial(four_kernel, heads), out_shape=(jax.Shap...]
where the time goes in v3:
time: 85.7 us; the launch traced here: 85.4 us
  Pallas kernels  72.6 us (85%)
  local copies, waits for them, and re-layouts  12.1 us (14%)
    pallas_call x1, Pallas kernels, four_shards(): pl.pallas_call(functools.partial(four_kernel, heads), out_shape=(jax.Shap...  72.6 us
    unnamed x4, local copies, waits for them, and re-layouts  12.1 us

profile of v3, /device:TPU:0, one launch (start us, length us, event | category | flops | bytes accessed | tf_op | source)
XLA Modules:
  0.0 85.4 jit_solution(15223949301851663485)
XLA Ops:
  0.6 1.9 %copy.15 = bf16[1,512,4,128]{3,1,2,0:T(8,128)(2,1)} copy(bf16[1,512,4,128]{3,2,1,0:T(4,128)(2,1)} %param.7) | data formatting | bytes 1048576 | tf_op args[1]
  2.5 3.5 %copy.14 = bf16[1,512,4,4,128]{4,1,3,2,0:T(8,128)(2,1)} copy(bf16[1,512,4,4,128]{4,3,2,1,0:T(4,128)(2,1)} %param.6) | data formatting | bytes 4194304 | tf_op args[0]
  6.0 72.6 %shard_map.77 = (bf16[4,512,128]{2,1,0:T(8,128)(2,1)}, bf16[4,4,512,128]{3,2,1,0:T(8,128)(2,1)}) custom-call(bf16[4,4,512,128]{3,2,1,0:T(8,128)(2,1)} %bitcast.17, bf16[4,512,128]{2,1,0:T(8,128)(2,1)} %bitcast.19, f32[1,2048]{1,0:T(1,128)} %weights.1, s32[1,2048]{1,0:T(1,128)} %items.1, s32[1,2048]{1,0:T(1,128)} %sessions.1, s32[3,1,4]{2,1,0:T(1,128)} %bitcast.21), custom_call_target="tpu_custom_call" | custom-call | tf_op jit(solution)/shard_map/pallas_call | solution.py:548
  78.6 2.2 %copy.10 = bf16[1,512,4,128]{3,2,1,0:T(4,128)(2,1)} copy(bf16[1,512,4,128]{3,1,2,0:T(8,128)(2,1)} %bitcast.20) | data formatting | bytes 1048576
  80.9 4.5 %copy.11 = bf16[1,512,4,4,128]{4,3,2,1,0:T(4,128)(2,1)} copy(bf16[1,512,4,4,128]{4,1,3,2,0:T(8,128)(2,1)} %bitcast.18) | data formatting | bytes 4194304

commit v4 on v3

--- a/solution.py
+++ b/solution.py
@@ -449,7 +449,8 @@
             query = qb[qi, h]
             grad = gb[qi, h]
 
-            def one_k(kj, carry):
+            def one_k(turn, carry):
+                kj = n_kv(qi) - 1 - turn
                 pair = qi * 2 + kj
                 for t in range(chunks):
                     part = pl.ds(t * step, step)
@@ -458,6 +459,13 @@
                     edges[part] = edge
                     dkv[kj, 0, part] += dot(edge, query, NN)
                     dkv[kj, 1, part] += dot(ptab[pair, h, part], grad, NN)
+
+                @pl.when((me == 1) & (qi == 2) & (kj == 1))
+                def _():
+                    dkvout[h, 0] = (dkv[1, 0] * scale).astype(jnp.bfloat16)
+                    dkvout[h, 1] = dkv[1, 1].astype(jnp.bfloat16)
+                    dkv_copy(h).start()
+
                 acc[...] += dot(kb[kj, h, 0], edges[...], TN)
                 return carry
 
@@ -477,12 +485,6 @@
             return carry
 
         lax.fori_loop(0, n_q, one_q, 0)
-
-        @pl.when(me == 1)
-        def _():
-            dkvout[h, 0] = (dkv[1, 0] * scale).astype(jnp.bfloat16)
-            dkvout[h, 1] = dkv[1, 1].astype(jnp.bfloat16)
-            dkv_copy(h).start()
 
         dkvown[h, 0] = dkv[0, 0] * scale
         dkvown[h, 1] = dkv[0, 1]

time: 85.7 us -> 85.7 us (level)
  no operation moved by 1% of the time
where the time goes in v4:
time: 85.7 us; the launch traced here: 85.4 us
  Pallas kernels  72.6 us (85%)
  local copies, waits for them, and re-layouts  12.1 us (14%)
    pallas_call x1, Pallas kernels, four_shards(): pl.pallas_call(functools.partial(four_kernel, heads), out_shape=(jax.Shap...  72.6 us
    unnamed x4, local copies, waits for them, and re-layouts  12.1 us

profile of v4, /device:TPU:0, one launch (start us, length us, event | category | flops | bytes accessed | tf_op | source)
XLA Modules:
  0.0 85.4 jit_solution(12187887922492519615)
XLA Ops:
  0.6 1.9 %copy.15 = bf16[1,512,4,128]{3,1,2,0:T(8,128)(2,1)} copy(bf16[1,512,4,128]{3,2,1,0:T(4,128)(2,1)} %param.7) | data formatting | bytes 1048576 | tf_op args[1]
  2.5 3.5 %copy.14 = bf16[1,512,4,4,128]{4,1,3,2,0:T(8,128)(2,1)} copy(bf16[1,512,4,4,128]{4,3,2,1,0:T(4,128)(2,1)} %param.6) | data formatting | bytes 4194304 | tf_op args[0]
  6.0 72.6 %shard_map.77 = (bf16[4,512,128]{2,1,0:T(8,128)(2,1)}, bf16[4,4,512,128]{3,2,1,0:T(8,128)(2,1)}) custom-call(bf16[4,4,512,128]{3,2,1,0:T(8,128)(2,1)} %bitcast.17, bf16[4,512,128]{2,1,0:T(8,128)(2,1)} %bitcast.19, f32[1,2048]{1,0:T(1,128)} %weights.1, s32[1,2048]{1,0:T(1,128)} %items.1, s32[1,2048]{1,0:T(1,128)} %sessions.1, s32[3,1,4]{2,1,0:T(1,128)} %bitcast.21), custom_call_target="tpu_custom_call" | custom-call | tf_op jit(solution)/shard_map/pallas_call | solution.py:550
  78.6 2.2 %copy.10 = bf16[1,512,4,128]{3,2,1,0:T(4,128)(2,1)} copy(bf16[1,512,4,128]{3,1,2,0:T(8,128)(2,1)} %bitcast.20) | data formatting | bytes 1048576
  80.9 4.5 %copy.11 = bf16[1,512,4,4,128]{4,3,2,1,0:T(4,128)(2,1)} copy(bf16[1,512,4,4,128]{4,1,3,2,0:T(8,128)(2,1)} %bitcast.18) | data formatting | bytes 4194304
